TPU v7x, 32 devices: a whole 2x2x4 slice. The times are simulated.
32 devices in a mesh: blk: 8 (over z, y), ulysses: 4 (over x, core).
Axes of the slice: x: 2, y: 2, z: 4, core: 2. Of those that a mesh axis runs over, the one named last changes fastest.
Arguments:
- queries: bfloat16 [192, 4096], P(('blk', 'ulysses')), may hold values from -8 to 8
- key_vectors: bfloat16 [192, 4096], P(('blk', 'ulysses')), may hold values from -8 to 8
- value_vectors: bfloat16 [192, 4096], P(('blk', 'ulysses')), may hold values from -12 to 12
- cotangent: bfloat16 [192, 4096], P(('blk', 'ulysses')), may hold values from -192 to 192
Outputs:
- grad_queries: bfloat16 [192, 4096], P(('blk', 'ulysses'))
- grad_keys: bfloat16 [192, 4096], P(('blk', 'ulysses'))
- grad_values: bfloat16 [192, 4096], P(('blk', 'ulysses'))
All inputs are finite; a program needn't handle non-finite values.
Results may differ from a plain program's by a relative error of at most 0.0067.
Values may be sent and summed in bfloat16 or wider, within the bound.
No kernel may reach another device: no remote copies, remote signals or barrier semaphores. Data moves between devices by JAX's collectives and lax.ppermute only.
A program may use at most 64 MiB of HBM per device.

v0:
```python
import math

import jax
import jax.numpy as jnp
from jax import lax
from jax.sharding import PartitionSpec as P

HEADS = 32
D_HEAD = 128


def scores(query_part, key_part, score_scale):
    return (
        jnp.einsum("qhd,khd->hqk", query_part, key_part, preferred_element_type=jnp.float32)
        * score_scale
    )


def local(queries, key_vectors, value_vectors, cotangent):
    ulysses_size = lax.axis_size("ulysses")
    head_dev = HEADS // ulysses_size
    score_scale = 1.0 / math.sqrt(D_HEAD)
    query_heads, key_heads, value_heads, grad_heads = (
        lax.all_to_all(queries, "ulysses", split_axis=1, concat_axis=0, tiled=True),
        lax.all_to_all(key_vectors, "ulysses", split_axis=1, concat_axis=0, tiled=True),
        lax.all_to_all(value_vectors, "ulysses", split_axis=1, concat_axis=0, tiled=True),
        lax.all_to_all(cotangent, "ulysses", split_axis=1, concat_axis=0, tiled=True),
    )
    local_rows = query_heads.shape[0]

    def split_heads(matrix):
        return matrix.reshape(matrix.shape[0], head_dev, D_HEAD)

    own_query = split_heads(query_heads)
    own_key = split_heads(key_heads)
    own_value = split_heads(value_heads)
    own_grad = split_heads(grad_heads)
    held_key, held_value = (
        lax.all_gather(key_heads, "blk", axis=0, tiled=True),
        lax.all_gather(value_heads, "blk", axis=0, tiled=True),
    )
    held_key = split_heads(held_key)
    held_value = split_heads(held_value)
    logits = scores(own_query, held_key, score_scale)
    grad_weights = jnp.einsum(
        "qhd,khd->hqk", own_grad, held_value, preferred_element_type=jnp.float32
    )
    block_top = jnp.max(logits, axis=2)
    exp_terms = jnp.exp(logits - block_top[:, :, None])
    row_total = jnp.sum(exp_terms, axis=2)
    row_sum = jnp.sum(exp_terms * grad_weights, axis=2)
    log_total = block_top + jnp.log(row_total)
    row_dot = row_sum / row_total
    all_log, all_dot = (
        lax.all_gather(log_total.T, "blk", axis=0, tiled=True),
        lax.all_gather(row_dot.T, "blk", axis=0, tiled=True),
    )
    logits = scores(own_query, held_key, score_scale)
    weights = jnp.exp(logits - log_total[:, :, None])
    grad_weights = jnp.einsum(
        "qhd,khd->hqk", own_grad, held_value, preferred_element_type=jnp.float32
    )
    grad_low = (weights * (grad_weights - row_dot[:, :, None])).astype(jnp.bfloat16)
    grad_query = jnp.einsum("hqk,khd->qhd", grad_low, held_key, preferred_element_type=jnp.float32)
    remote_query = split_heads(lax.all_gather(query_heads, "blk", axis=0, tiled=True))
    remote_grad = split_heads(lax.all_gather(grad_heads, "blk", axis=0, tiled=True))
    logits = scores(remote_query, own_key, score_scale)
    weights = jnp.exp(logits - all_log.T[:, :, None])
    grad_weights = jnp.einsum(
        "qhd,khd->hqk", remote_grad, own_value, preferred_element_type=jnp.float32
    )
    grad_low = (weights * (grad_weights - all_dot.T[:, :, None])).astype(jnp.bfloat16)
    weights_low = weights.astype(jnp.bfloat16)
    grad_key = jnp.einsum(
        "hqk,qhd->khd", grad_low, remote_query, preferred_element_type=jnp.float32
    )
    grad_value = jnp.einsum(
        "hqk,qhd->khd", weights_low, remote_grad, preferred_element_type=jnp.float32
    )
    grad_key, grad_value = (grad_key, grad_value)

    def to_rows(summed, factor):
        return (summed * factor).astype(jnp.bfloat16).reshape(local_rows, head_dev * D_HEAD)

    return (
        lax.all_to_all(
            to_rows(grad_query, score_scale), "ulysses", split_axis=0, concat_axis=1, tiled=True
        ),
        lax.all_to_all(
            to_rows(grad_key, score_scale), "ulysses", split_axis=0, concat_axis=1, tiled=True
        ),
        lax.all_to_all(
            to_rows(grad_value, 1.0), "ulysses", split_axis=0, concat_axis=1, tiled=True
        ),
    )


def solution(mesh):
    placed = (
        P(("blk", "ulysses"), None),
        P(("blk", "ulysses"), None),
        P(("blk", "ulysses"), None),
        P(("blk", "ulysses"), None),
    )
    return jax.shard_map(
        local,
        mesh=mesh,
        in_specs=placed,
        out_specs=(
            P(("blk", "ulysses"), None),
            P(("blk", "ulysses"), None),
            P(("blk", "ulysses"), None),
        ),
        check_vma=False,
    )
```

profile of v0, /device:TPU:1, one launch (start us, length us, event | category | flops | bytes accessed | tf_op | source)
XLA Modules:
  0.0 238.1 jit_solution(16332870402772391413)
XLA Ops:
  0.6 7.7 %all_to_all.133 = bf16[6,4,1024]{2,0,1:T(8,128)(2,1)S(1)} all-to-all(bf16[6,4,1024]{2,0,1:T(8,128)(2,1)} %bitcast.95), channel_id=1, replica_groups=mesh['blk'=8,'ulysses'=4] {'ulysses'}, dimensions={1} | all-to-all | bytes 98304 | tf_op jit(solution)/shard_map/all_to_all | solution.py:24
  8.3 6.6 %all_to_all.134 = bf16[6,4,1024]{2,0,1:T(8,128)(2,1)S(1)} all-to-all(bf16[6,4,1024]{2,0,1:T(8,128)(2,1)S(1)} %bitcast.96), channel_id=1, replica_groups=mesh['blk'=8,'ulysses'=4] {'ulysses'}, dimensions={1} | all-to-all | bytes 98304 | tf_op jit(solution)/shard_map/all_to_all | solution.py:25
  14.9 6.5 %all_to_all.135 = bf16[6,4,1024]{2,0,1:T(8,128)(2,1)S(1)} all-to-all(bf16[6,4,1024]{2,0,1:T(8,128)(2,1)S(1)} %bitcast.97), channel_id=1, replica_groups=mesh['blk'=8,'ulysses'=4] {'ulysses'}, dimensions={1} | all-to-all | bytes 98304 | tf_op jit(solution)/shard_map/all_to_all | solution.py:26
  21.4 4.1 %all-to-all-start.2 = ((bf16[6,4,1024]{2,0,1:T(8,128)(2,1)}), bf16[6,4,1024]{2,0,1:T(8,128)(2,1)S(1)}, u32[]{:S(2)}, u32[]{:S(2)}) async-start(bf16[6,4,1024]{2,0,1:T(8,128)(2,1)} %bitcast.4), calls=%async_computation.2 | async-start | bytes 131072 | tf_op jit(solution)/shard_map/all_to_all | solution.py:27
  25.9 2.9 %all-to-all-done.2 = bf16[6,4,1024]{2,0,1:T(8,128)(2,1)S(1)} async-done(((bf16[6,4,1024]{2,0,1:T(8,128)(2,1)}), bf16[6,4,1024]{2,0,1:T(8,128)(2,1)S(1)}, u32[]{:S(2)}, u32[]{:S(2)}) %all-to-all-start.2) | async-done | bytes 49184 | tf_op jit(solution)/shard_map/all_to_all | solution.py:27
  28.9 26.0 %all_gather.18 = bf16[192,1024]{1,0:T(8,128)(2,1)S(1)} all-gather(bf16[24,1024]{1,0:T(8,128)(2,1)S(1)} %all_to_all.104), channel_id=1, replica_groups=mesh['blk'=8,'ulysses'=4] {'blk'}, dimensions={0}, use_global_device_ids=true | all-gather | bytes 442368 | tf_op jit(solution)/shard_map/all_gather | solution.py:39
  54.9 25.4 %all_gather.19 = bf16[192,1024]{1,0:T(8,128)(2,1)S(1)} all-gather(bf16[24,1024]{1,0:T(8,128)(2,1)S(1)} %all_to_all.111), channel_id=1, replica_groups=mesh['blk'=8,'ulysses'=4] {'blk'}, dimensions={0}, use_global_device_ids=true | all-gather | bytes 442368 | tf_op jit(solution)/shard_map/all_gather | solution.py:40
  80.7 0.4 fusion.28
  81.4 0.7 all_to_all.112
  82.1 15.7 %all-to-all-start.4 = ((bf16[4,6,1024]{2,1,0:T(8,128)(2,1)}), bf16[4,6,1024]{2,1,0:T(8,128)(2,1)S(1)}, u32[]{:S(2)}, u32[]{:S(2)}) async-start(bf16[4,6,1024]{2,1,0:T(8,128)(2,1)} %all_to_all.112), calls=%async_computation.4 | async-start | bytes 131072 | tf_op jit(solution)/shard_map/all_to_all | solution.py:86
  97.8 24.0 %all-gather = f32[8,24,8]{1,2,0:T(8,128)S(1)} all-gather(f32[1,24,8]{1,2,0:T(8,128)S(1)} %bitcast.99), channel_id=1, replica_groups=mesh['blk'=8,'ulysses'=4] {'blk'}, dimensions={0}, use_global_device_ids=true | all-gather | bytes 6912 | tf_op jit(solution)/shard_map/all_gather | solution.py:55
  121.9 25.2 %all_gather.20 = bf16[192,1024]{1,0:T(8,128)(2,1)S(1)} all-gather(bf16[24,1024]{1,0:T(8,128)(2,1)S(1)} %all_to_all.116), channel_id=1, replica_groups=mesh['blk'=8,'ulysses'=4] {'blk'}, dimensions={0}, use_global_device_ids=true | all-gather | bytes 442368 | tf_op jit(solution)/shard_map/all_gather | solution.py:65
  147.1 24.1 %all-gather.1 = f32[8,24,8]{1,2,0:T(8,128)S(1)} all-gather(f32[1,24,8]{1,2,0:T(8,128)S(1)} %bitcast.98), channel_id=1, replica_groups=mesh['blk'=8,'ulysses'=4] {'blk'}, dimensions={0}, use_global_device_ids=true | all-gather | bytes 6912 | tf_op jit(solution)/shard_map/all_gather | solution.py:56
  171.3 24.6 %all_gather.22 = bf16[192,1024]{1,0:T(8,128)(2,1)S(1)} all-gather(bf16[24,1024]{1,0:T(8,128)(2,1)S(1)} %all_to_all.117), channel_id=1, replica_groups=mesh['blk'=8,'ulysses'=4] {'blk'}, dimensions={0}, use_global_device_ids=true | all-gather | bytes 442368 | tf_op jit(solution)/shard_map/all_gather | solution.py:66
  196.2 0.4 fusion.8
  196.7 0.7 all_to_all.118
  197.4 28.1 %all-to-all-start.5 = ((bf16[4,6,1024]{2,1,0:T(8,128)(2,1)}), bf16[4,6,1024]{2,1,0:T(8,128)(2,1)S(1)}, u32[]{:S(2)}, u32[]{:S(2)}) async-start(bf16[4,6,1024]{2,1,0:T(8,128)(2,1)} %all_to_all.118), calls=%async_computation.5 | async-start | bytes 131072 | tf_op jit(solution)/shard_map/all_to_all | solution.py:89
  225.8 0.7 all_to_all.122
  226.5 2.3 all-to-all-done.5
  228.8 4.1 %all-to-all-start.6 = ((bf16[4,6,1024]{2,1,0:T(8,128)(2,1)}), bf16[4,6,1024]{2,1,0:T(8,128)(2,1)S(1)}, u32[]{:S(2)}, u32[]{:S(2)}) async-start(bf16[4,6,1024]{2,1,0:T(8,128)(2,1)} %all_to_all.122), calls=%async_computation.6 | async-start | bytes 131072 | tf_op jit(solution)/shard_map/all_to_all | solution.py:92
  232.9 3.3 %all-to-all-done.6 = bf16[4,6,1024]{2,1,0:T(8,128)(2,1)S(1)} async-done(((bf16[4,6,1024]{2,1,0:T(8,128)(2,1)}), bf16[4,6,1024]{2,1,0:T(8,128)(2,1)S(1)}, u32[]{:S(2)}, u32[]{:S(2)}) %all-to-all-start.6) | async-done | bytes 49184 | tf_op jit(solution)/shard_map/all_to_all | solution.py:92
  236.2 0.6 copy.97
  236.8 0.6 copy.98
  237.4 0.6 copy.99
  (25 shorter events, 1.9 us)
Async XLA Ops:
  0.6 7.7 %copy-start = (bf16[6,4096]{1,0:T(8,128)(2,1)S(1)}, bf16[6,4096]{1,0:T(8,128)(2,1)}, u32[]{:S(2)}) copy-start(bf16[6,4096]{1,0:T(8,128)(2,1)} %param.5) | copy-start | bytes 147460
  8.3 6.6 %copy-start.1 = (bf16[6,4096]{1,0:T(8,128)(2,1)S(1)}, bf16[6,4096]{1,0:T(8,128)(2,1)}, u32[]{:S(2)}) copy-start(bf16[6,4096]{1,0:T(8,128)(2,1)} %param.6) | copy-start | bytes 147460
  21.4 7.4 %all-to-all-start.2 = ((bf16[6,4,1024]{2,0,1:T(8,128)(2,1)}), bf16[6,4,1024]{2,0,1:T(8,128)(2,1)S(1)}, u32[]{:S(2)}, u32[]{:S(2)}) async-start(bf16[6,4,1024]{2,0,1:T(8,128)(2,1)} %bitcast.4), calls=%async_computation.2 | async-start | bytes 131072 | tf_op jit(solution)/shard_map/all_to_all | solution.py:27
  82.1 115.3 %all-to-all-start.4 = ((bf16[4,6,1024]{2,1,0:T(8,128)(2,1)}), bf16[4,6,1024]{2,1,0:T(8,128)(2,1)S(1)}, u32[]{:S(2)}, u32[]{:S(2)}) async-start(bf16[4,6,1024]{2,1,0:T(8,128)(2,1)} %all_to_all.112), calls=%async_computation.4 | async-start | bytes 131072 | tf_op jit(solution)/shard_map/all_to_all | solution.py:86
  197.4 31.4 %all-to-all-start.5 = ((bf16[4,6,1024]{2,1,0:T(8,128)(2,1)}), bf16[4,6,1024]{2,1,0:T(8,128)(2,1)S(1)}, u32[]{:S(2)}, u32[]{:S(2)}) async-start(bf16[4,6,1024]{2,1,0:T(8,128)(2,1)} %all_to_all.118), calls=%async_computation.5 | async-start | bytes 131072 | tf_op jit(solution)/shard_map/all_to_all | solution.py:89
  228.8 7.4 %all-to-all-start.6 = ((bf16[4,6,1024]{2,1,0:T(8,128)(2,1)}), bf16[4,6,1024]{2,1,0:T(8,128)(2,1)S(1)}, u32[]{:S(2)}, u32[]{:S(2)}) async-start(bf16[4,6,1024]{2,1,0:T(8,128)(2,1)} %all_to_all.122), calls=%async_computation.6 | async-start | bytes 131072 | tf_op jit(solution)/shard_map/all_to_all | solution.py:92
where the time goes:
time: 240 us; the launch traced here: 238 us
  blocking collectives  170 us (71%)
  starting transfers between devices  52.1 us (22%)
  waiting for transfers between devices  8.49 us (4%)
  local copies, waits for them, and re-layouts  4.64 us (2%)
    all_to_all x1, starting transfers between devices, local(): lax.all_to_all(to_rows(grad_key, score_scale), 'ulysses', split_axis=0, c...  28.1 us
    all_gather x1, blocking collectives, local(): lax.all_gather(key_heads, 'blk', axis=0, tiled=True)  26 us
    all_gather x1, blocking collectives, local(): lax.all_gather(value_heads, 'blk', axis=0, tiled=True)  25.4 us
    all_gather x1, blocking collectives, local(): lax.all_gather(query_heads, 'blk', axis=0, tiled=True)  25.2 us
    all_gather x1, blocking collectives, local(): lax.all_gather(grad_heads, 'blk', axis=0, tiled=True)  24.6 us
    all_gather x1, blocking collectives, local(): lax.all_gather(row_dot.T, 'blk', axis=0, tiled=True)  24.1 us
    all_gather x1, blocking collectives, local(): lax.all_gather(log_total.T, 'blk', axis=0, tiled=True)  24 us
    all_to_all x1, starting transfers between devices, local(): lax.all_to_all(to_rows(grad_query, score_scale), 'ulysses', split_axis=0,...  15.7 us
  transfers between devices with their start and end apart: 4, of which 3 were waited for; matrix products, arithmetic and copies ran while one was open for 1% of the time, Pallas kernels for 0%

commit v1 on v0

--- a/solution.py
+++ b/solution.py
@@ -3,10 +3,88 @@
 import jax
 import jax.numpy as jnp
 from jax import lax
+from jax.experimental import pallas as pl
+from jax.experimental.pallas import tpu as pltpu
 from jax.sharding import PartitionSpec as P
 
 HEADS = 32
 D_HEAD = 128
+AXES = ("blk", "ulysses")
+VMEM = pl.BlockSpec(memory_space=pltpu.VMEM)
+
+
+def pack_kernel(query_ref, key_ref, value_ref, grad_ref, out_ref):
+    rows = query_ref.shape[0]
+    heads = out_ref.shape[0]
+    for head in range(heads):
+        columns = slice(head * D_HEAD, (head + 1) * D_HEAD)
+        parts = [
+            ref[:, columns].astype(jnp.float32)
+            for ref in (query_ref, key_ref, value_ref, grad_ref)
+        ]
+        out_ref[head] = jnp.concatenate(parts, axis=0).astype(jnp.bfloat16)
+
+
+def dot(left, right, left_dim, right_dim):
+    return lax.dot_general(
+        left, right, (((left_dim,), (right_dim,)), ((), ())), preferred_element_type=jnp.float32
+    )
+
+
+def head_kernel(rows, in_ref, out_ref):
+    senders = in_ref.shape[0]
+    score_scale = 1.0 / math.sqrt(D_HEAD)
+    blocks = [in_ref[sender].astype(jnp.float32) for sender in range(senders)]
+
+    def gathered(which):
+        return jnp.concatenate(
+            [block[which * rows : (which + 1) * rows] for block in blocks], axis=0
+        ).astype(jnp.bfloat16)
+
+    query, key, value, grad = (gathered(which) for which in range(4))
+    logits = dot(query, key, 1, 1) * score_scale
+    top = jnp.max(logits, axis=1, keepdims=True)
+    terms = jnp.exp(logits - top)
+    weights = terms / jnp.sum(terms, axis=1, keepdims=True)
+    grad_weights = dot(grad, value, 1, 1)
+    row_dot = jnp.sum(weights * grad_weights, axis=1, keepdims=True)
+    grad_low = (weights * (grad_weights - row_dot)).astype(jnp.bfloat16)
+    weights_low = weights.astype(jnp.bfloat16)
+    grad_query = dot(grad_low, key, 1, 0) * score_scale
+    grad_key = dot(grad_low, query, 0, 0) * score_scale
+    grad_value = dot(weights_low, grad, 0, 0)
+    for sender in range(senders):
+        own = slice(sender * rows, (sender + 1) * rows)
+        out_ref[sender, : 3 * rows] = jnp.concatenate(
+            [grad_query[own], grad_key[own], grad_value[own]], axis=0
+        ).astype(jnp.bfloat16)
+    out_ref[:, 3 * rows :] = jnp.zeros_like(out_ref[:, 3 * rows :])
+
+
+def unpack_kernel(in_ref, query_ref, key_ref, value_ref):
+    rows = query_ref.shape[0]
+    for head in range(in_ref.shape[0]):
+        block = in_ref[head].astype(jnp.float32)
+        columns = slice(head * D_HEAD, (head + 1) * D_HEAD)
+        for which, ref in enumerate((query_ref, key_ref, value_ref)):
+            ref[:, columns] = block[which * rows : (which + 1) * rows].astype(jnp.bfloat16)
+
+
+def by_head(queries, key_vectors, value_vectors, cotangent):
+    rows = queries.shape[0]
+    sent = jax.ShapeDtypeStruct((HEADS, 4 * rows, D_HEAD), jnp.bfloat16)
+    packed = pl.pallas_call(
+        pack_kernel, out_shape=sent, in_specs=[VMEM] * 4, out_specs=VMEM
+    )(queries, key_vectors, value_vectors, cotangent)
+    held = lax.all_to_all(packed, AXES, split_axis=0, concat_axis=0, tiled=True)
+    back = pl.pallas_call(
+        lambda *refs: head_kernel(rows, *refs), out_shape=sent, in_specs=[VMEM], out_specs=VMEM
+    )(held)
+    back = lax.all_to_all(back, AXES, split_axis=0, concat_axis=0, tiled=True)
+    out = jax.ShapeDtypeStruct(queries.shape, jnp.bfloat16)
+    return pl.pallas_call(
+        unpack_kernel, out_shape=(out,) * 3, in_specs=[VMEM], out_specs=(VMEM,) * 3
+    )(back)
 
 
 def scores(query_part, key_part, score_scale):
@@ -16,7 +94,7 @@
     )
 
 
-def local(queries, key_vectors, value_vectors, cotangent):
+def by_block(queries, key_vectors, value_vectors, cotangent):
     ulysses_size = lax.axis_size("ulysses")
     head_dev = HEADS // ulysses_size
     score_scale = 1.0 / math.sqrt(D_HEAD)
@@ -102,6 +180,7 @@
         P(("blk", "ulysses"), None),
         P(("blk", "ulysses"), None),
     )
+    local = by_head if mesh.size == HEADS else by_block
     return jax.shard_map(
         local,
         mesh=mesh,

time: 240 us -> 35.2 us (0.15)
  blocking collectives: 170 us -> 28.6 us
  starting transfers between devices: 52.1 us -> 0 us
  waiting for transfers between devices: 8.49 us -> 0 us
  Pallas kernels: 0 us -> 5.63 us
  local copies, waits for them, and re-layouts: 4.64 us -> 0 us
    all_gather x6 -> x0, blocking collectives: 149 us -> none  [the longest x1 26 us: local(): lax.all_gather(key_heads, 'blk', axis=0, tiled=True)]
    all_to_all x4 -> x0, starting transfers between devices: 52.1 us -> none  [the longest x1 28.1 us: local(): lax.all_to_all(to_rows(grad_key, score_scale), 'ulysses', split_axis=0, c...]
    all_to_all x4 -> x0, waiting for transfers between devices: 8.49 us -> none  [the longest x1 3.26 us: local(): lax.all_to_all(to_rows(grad_value, 1.0), 'ulysses', split_axis=0, concat_...]
    all_to_all x3 -> x2, blocking collectives: 20.7 us -> 28.6 us  [the longest x1 16.4 us: by_head(): held = lax.all_to_all(packed, AXES, split_axis=0, concat_axis=0, tiled=True)]
    pallas_call x0 -> x3, Pallas kernels: none -> 5.63 us  [the longest x1 2.31 us: by_head(): pl.pallas_call(lambda *refs: head_kernel(rows, *refs), out_shape=sent, in...]
  transfers between devices with their start and end apart: 4 -> 0, of which waited for: 3 -> 0; matrix products, arithmetic and copies ran while one was open for 1% -> 0% of each run, Pallas kernels for 0% -> 0%
where the time goes in v1:
time: 35.2 us; the launch traced here: 34.9 us
  blocking collectives  28.6 us (81%)
  Pallas kernels  5.63 us (16%)
  between operations  0.63 us (2%)
    all_to_all x1, blocking collectives, by_head(): held = lax.all_to_all(packed, AXES, split_axis=0, concat_axis=0, tiled=True)  16.4 us
    all_to_all x1, blocking collectives, by_head(): back = lax.all_to_all(back, AXES, split_axis=0, concat_axis=0, tiled=True)  12.2 us
    pallas_call x1, Pallas kernels, by_head(): pl.pallas_call(lambda *refs: head_kernel(rows, *refs), out_shape=sent, in...  2.31 us
    pallas_call x1, Pallas kernels, by_head(): pl.pallas_call(pack_kernel, out_shape=sent, in_specs=[VMEM] * 4, out_spec...  1.67 us
    pallas_call x1, Pallas kernels, by_head(): pl.pallas_call(unpack_kernel, out_shape=(out,) * 3, in_specs=[VMEM], out_...  1.65 us

profile of v1, /device:TPU:1, one launch (start us, length us, event | category | flops | bytes accessed | tf_op | source)
XLA Modules:
  0.0 34.9 jit_solution(13771874255953295665)
XLA Ops:
  0.6 1.7 %shard_map.67 = bf16[32,24,128]{2,1,0:T(8,128)(2,1)} custom-call(bf16[6,4096]{1,0:T(8,128)(2,1)} %query_ref.1, bf16[6,4096]{1,0:T(8,128)(2,1)} %key_ref.1, bf16[6,4096]{1,0:T(8,128)(2,1)} %value_ref.1, bf16[6,4096]{1,0:T(8,128)(2,1)} %grad_ref.1), custom_call_target="tpu_custom_call" | custom-call | tf_op jit(solution)/shard_map/pallas_call | solution.py:76
  2.3 16.4 %all_to_all.10.refs_0_ = bf16[32,24,128]{2,1,0:T(8,128)(2,1)} all-to-all(bf16[32,24,128]{2,1,0:T(8,128)(2,1)} %shard_map.67), channel_id=1, replica_groups=mesh['blk'=8,'ulysses'=4] {'blk','ulysses'}, dimensions={0} | all-to-all | bytes 393216 | tf_op jit(solution)/shard_map/all_to_all | solution.py:79
  18.7 2.3 %shard_map.68 = bf16[32,24,128]{2,1,0:T(8,128)(2,1)} custom-call(bf16[32,24,128]{2,1,0:T(8,128)(2,1)} %all_to_all.10.refs_0_), custom_call_target="tpu_custom_call" | custom-call | tf_op jit(solution)/shard_map/pallas_call | solution.py:80
  21.1 12.2 %all_to_all.11.in_ref = bf16[32,24,128]{2,1,0:T(8,128)(2,1)} all-to-all(bf16[32,24,128]{2,1,0:T(8,128)(2,1)} %shard_map.68), channel_id=1, replica_groups=mesh['blk'=8,'ulysses'=4] {'blk','ulysses'}, dimensions={0} | all-to-all | bytes 393216 | tf_op jit(solution)/shard_map/all_to_all | solution.py:83
  33.2 1.6 %shard_map.69 = (bf16[6,4096]{1,0:T(8,128)(2,1)}, bf16[6,4096]{1,0:T(8,128)(2,1)}, bf16[6,4096]{1,0:T(8,128)(2,1)}) custom-call(bf16[32,24,128]{2,1,0:T(8,128)(2,1)} %all_to_all.11.in_ref), custom_call_target="tpu_custom_call" | custom-call | tf_op jit(solution)/shard_map/pallas_call | solution.py:85

commit v2 on v1

--- a/solution.py
+++ b/solution.py
@@ -10,18 +10,23 @@
 HEADS = 32
 D_HEAD = 128
 AXES = ("blk", "ulysses")
+HBM = pl.BlockSpec(memory_space=pltpu.HBM)
 VMEM = pl.BlockSpec(memory_space=pltpu.VMEM)
-
-
-def pack_kernel(query_ref, key_ref, value_ref, grad_ref, out_ref):
-    rows = query_ref.shape[0]
-    heads = out_ref.shape[0]
-    for head in range(heads):
+PARAMS = pltpu.CompilerParams(vmem_limit_bytes=8 * 2**20)
+
+
+def pack_kernel(query_ref, key_ref, value_ref, grad_ref, out_ref, held, arrived):
+    copies = [
+        pltpu.make_async_copy(ref, held.at[which], arrived.at[which])
+        for which, ref in enumerate((query_ref, key_ref, value_ref, grad_ref))
+    ]
+    for copy in copies:
+        copy.start()
+    for copy in copies:
+        copy.wait()
+    for head in range(out_ref.shape[0]):
         columns = slice(head * D_HEAD, (head + 1) * D_HEAD)
-        parts = [
-            ref[:, columns].astype(jnp.float32)
-            for ref in (query_ref, key_ref, value_ref, grad_ref)
-        ]
+        parts = [held[which, :, columns].astype(jnp.float32) for which in range(4)]
         out_ref[head] = jnp.concatenate(parts, axis=0).astype(jnp.bfloat16)
 
 
@@ -50,41 +55,73 @@
     row_dot = jnp.sum(weights * grad_weights, axis=1, keepdims=True)
     grad_low = (weights * (grad_weights - row_dot)).astype(jnp.bfloat16)
     weights_low = weights.astype(jnp.bfloat16)
-    grad_query = dot(grad_low, key, 1, 0) * score_scale
-    grad_key = dot(grad_low, query, 0, 0) * score_scale
-    grad_value = dot(weights_low, grad, 0, 0)
-    for sender in range(senders):
-        own = slice(sender * rows, (sender + 1) * rows)
-        out_ref[sender, : 3 * rows] = jnp.concatenate(
-            [grad_query[own], grad_key[own], grad_value[own]], axis=0
-        ).astype(jnp.bfloat16)
-    out_ref[:, 3 * rows :] = jnp.zeros_like(out_ref[:, 3 * rows :])
+    grads = (
+        dot(grad_low, key, 1, 0) * score_scale,
+        dot(grad_low, query, 0, 0) * score_scale,
+        dot(weights_low, grad, 0, 0),
+    )
+    out_ref[...] = jnp.concatenate(
+        [
+            total[sender * rows : (sender + 1) * rows]
+            for sender in range(senders)
+            for total in grads
+        ],
+        axis=0,
+    ).astype(jnp.bfloat16)
 
 
 def unpack_kernel(in_ref, query_ref, key_ref, value_ref):
     rows = query_ref.shape[0]
-    for head in range(in_ref.shape[0]):
-        block = in_ref[head].astype(jnp.float32)
-        columns = slice(head * D_HEAD, (head + 1) * D_HEAD)
-        for which, ref in enumerate((query_ref, key_ref, value_ref)):
-            ref[:, columns] = block[which * rows : (which + 1) * rows].astype(jnp.bfloat16)
+    heads = in_ref.shape[0] // (3 * rows)
+    received = in_ref[...].astype(jnp.float32)
+    for which, ref in enumerate((query_ref, key_ref, value_ref)):
+        for head in range(heads):
+            first = (3 * head + which) * rows
+            columns = slice(head * D_HEAD, (head + 1) * D_HEAD)
+            ref[:, columns] = received[first : first + rows].astype(jnp.bfloat16)
 
 
 def by_head(queries, key_vectors, value_vectors, cotangent):
     rows = queries.shape[0]
-    sent = jax.ShapeDtypeStruct((HEADS, 4 * rows, D_HEAD), jnp.bfloat16)
     packed = pl.pallas_call(
-        pack_kernel, out_shape=sent, in_specs=[VMEM] * 4, out_specs=VMEM
-    )(queries, key_vectors, value_vectors, cotangent)
+        pack_kernel,
+        out_shape=jax.ShapeDtypeStruct((HEADS, 4 * rows, D_HEAD), jnp.bfloat16),
+        in_specs=[HBM] * 4,
+        out_specs=VMEM,
+        scratch_shapes=[
+            pltpu.VMEM((4,) + queries.shape, jnp.bfloat16),
+            pltpu.SemaphoreType.DMA((4,)),
+        ],
+        compiler_params=PARAMS,
+    )(*(
+        pltpu.with_memory_space_constraint(array, pltpu.HBM)
+        for array in (queries, key_vectors, value_vectors, cotangent)
+    ))
     held = lax.all_to_all(packed, AXES, split_axis=0, concat_axis=0, tiled=True)
+    grads = jax.ShapeDtypeStruct((HEADS * 3 * rows, D_HEAD), jnp.bfloat16)
     back = pl.pallas_call(
-        lambda *refs: head_kernel(rows, *refs), out_shape=sent, in_specs=[VMEM], out_specs=VMEM
+        lambda *refs: head_kernel(rows, *refs),
+        out_shape=grads,
+        in_specs=[VMEM],
+        out_specs=VMEM,
+        compiler_params=PARAMS,
     )(held)
-    back = lax.all_to_all(back, AXES, split_axis=0, concat_axis=0, tiled=True)
+    pair = math.gcd(rows, 2)
+    back = lax.all_to_all(
+        back.reshape(HEADS, 3 * rows // pair, pair, D_HEAD),
+        AXES,
+        split_axis=0,
+        concat_axis=0,
+        tiled=True,
+    )
     out = jax.ShapeDtypeStruct(queries.shape, jnp.bfloat16)
     return pl.pallas_call(
-        unpack_kernel, out_shape=(out,) * 3, in_specs=[VMEM], out_specs=(VMEM,) * 3
-    )(back)
+        unpack_kernel,
+        out_shape=(out,) * 3,
+        in_specs=[VMEM],
+        out_specs=(VMEM,) * 3,
+        compiler_params=PARAMS,
+    )(back.reshape(grads.shape))
 
 
 def scores(query_part, key_part, score_scale):

time: 35.2 us -> 30.2 us (0.86)
  Pallas kernels: 5.63 us -> 2.44 us
  blocking collectives: 28.6 us -> 26.8 us
    pallas_call x2, Pallas kernels: 3.98 us -> 1.73 us  [the longest x1 1.02 us: by_head(): pl.pallas_call(pack_kernel, out_shape=jax.ShapeDtypeStruct((HEADS, 4 * ro...]
    all_to_all x1, blocking collectives: 12.2 us -> 10.6 us  [by_head(): lax.all_to_all(back.reshape(HEADS, 3 * rows // pair, pair, D_HEAD), AXES,...]
    pallas_call x1, Pallas kernels: 1.65 us -> 0.71 us  [by_head(): pl.pallas_call(unpack_kernel, out_shape=(out,) * 3, in_specs=[VMEM], out_...]
where the time goes in v2:
time: 30.2 us; the launch traced here: 29.9 us
  blocking collectives  26.8 us (89%)
  Pallas kernels  2.44 us (8%)
  between operations  0.65 us (2%)
    all_to_all x1, blocking collectives, by_head(): held = lax.all_to_all(packed, AXES, split_axis=0, concat_axis=0, tiled=True)  16.1 us
    all_to_all x1, blocking collectives, by_head(): lax.all_to_all(back.reshape(HEADS, 3 * rows // pair, pair, D_HEAD), AXES,...  10.6 us
    pallas_call x1, Pallas kernels, by_head(): pl.pallas_call(pack_kernel, out_shape=jax.ShapeDtypeStruct((HEADS, 4 * ro...  1.02 us
    pallas_call x1, Pallas kernels, by_head(): pl.pallas_call(unpack_kernel, out_shape=(out,) * 3, in_specs=[VMEM], out_...  0.71 us
    pallas_call x1, Pallas kernels, by_head(): pl.pallas_call(lambda *refs: head_kernel(rows, *refs), out_shape=grads, i...  0.71 us

profile of v2, /device:TPU:1, one launch (start us, length us, event | category | flops | bytes accessed | tf_op | source)
XLA Modules:
  0.0 29.9 jit_solution(1996008373243970107)
XLA Ops:
  0.6 1.0 %shard_map.67 = bf16[32,24,128]{2,1,0:T(8,128)(2,1)S(1)} custom-call(bf16[6,4096]{1,0:T(8,128)(2,1)} %query_ref.1, bf16[6,4096]{1,0:T(8,128)(2,1)} %key_ref.1, bf16[6,4096]{1,0:T(8,128)(2,1)} %value_ref.1, bf16[6,4096]{1,0:T(8,128)(2,1)} %grad_ref.1), custom_call_target="tpu_custom_call" | custom-call | tf_op jit(solution)/shard_map/pallas_call | solution.py:86
  1.7 16.1 %all_to_all.10.refs_0_ = bf16[32,24,128]{2,1,0:T(8,128)(2,1)S(1)} all-to-all(bf16[32,24,128]{2,1,0:T(8,128)(2,1)S(1)} %shard_map.67), channel_id=1, replica_groups=mesh['blk'=8,'ulysses'=4] {'blk','ulysses'}, dimensions={0} | all-to-all | bytes 393216 | tf_op jit(solution)/shard_map/all_to_all | solution.py:100
  17.8 0.7 %shard_map.68 = bf16[576,128]{1,0:T(8,128)(2,1)S(1)} custom-call(bf16[32,24,128]{2,1,0:T(8,128)(2,1)S(1)} %all_to_all.10.refs_0_), custom_call_target="tpu_custom_call" | custom-call | tf_op jit(solution)/shard_map/pallas_call | solution.py:102
  18.5 10.6 %all_to_all.11 = bf16[32,9,2,128]{3,2,1,0:T(2,128)(2,1)S(1)} all-to-all(bf16[32,9,2,128]{3,2,1,0:T(2,128)(2,1)S(1)} %bitcast.3), channel_id=1, replica_groups=mesh['blk'=8,'ulysses'=4] {'blk','ulysses'}, dimensions={0} | all-to-all | bytes 294912 | tf_op jit(solution)/shard_map/all_to_all | solution.py:110
  29.1 0.7 %shard_map.69 = (bf16[6,4096]{1,0:T(8,128)(2,1)}, bf16[6,4096]{1,0:T(8,128)(2,1)}, bf16[6,4096]{1,0:T(8,128)(2,1)}) custom-call(bf16[576,128]{1,0:T(8,128)(2,1)S(1)} %bitcast.2), custom_call_target="tpu_custom_call" | custom-call | tf_op jit(solution)/shard_map/pallas_call | solution.py:118

commit v3 on v2

--- a/solution.py
+++ b/solution.py
@@ -2,6 +2,7 @@
 
 import jax
 import jax.numpy as jnp
+import numpy as np
 from jax import lax
 from jax.experimental import pallas as pl
 from jax.experimental.pallas import tpu as pltpu
@@ -81,6 +82,20 @@
             ref[:, columns] = received[first : first + rows].astype(jnp.bfloat16)
 
 
+def places():
+    blk_size, ulysses_size = lax.axis_size("blk"), lax.axis_size("ulysses")
+    index = np.arange(blk_size * ulysses_size)
+    if blk_size % 2 == 0 and ulysses_size % 2 == 0:
+        index = index.reshape(blk_size // 2, 2, ulysses_size // 2, 2).transpose(1, 3, 2, 0)
+    return [[int(device) for device in index.reshape(-1)]]
+
+
+def exchange(chunks):
+    return lax.all_to_all(
+        chunks, AXES, split_axis=0, concat_axis=0, tiled=True, axis_index_groups=places()
+    )
+
+
 def by_head(queries, key_vectors, value_vectors, cotangent):
     rows = queries.shape[0]
     packed = pl.pallas_call(
@@ -93,11 +108,13 @@
             pltpu.SemaphoreType.DMA((4,)),
         ],
         compiler_params=PARAMS,
-    )(*(
-        pltpu.with_memory_space_constraint(array, pltpu.HBM)
-        for array in (queries, key_vectors, value_vectors, cotangent)
-    ))
-    held = lax.all_to_all(packed, AXES, split_axis=0, concat_axis=0, tiled=True)
+    )(
+        *(
+            pltpu.with_memory_space_constraint(array, pltpu.HBM)
+            for array in (queries, key_vectors, value_vectors, cotangent)
+        )
+    )
+    held = exchange(packed)
     grads = jax.ShapeDtypeStruct((HEADS * 3 * rows, D_HEAD), jnp.bfloat16)
     back = pl.pallas_call(
         lambda *refs: head_kernel(rows, *refs),
@@ -107,13 +124,7 @@
         compiler_params=PARAMS,
     )(held)
     pair = math.gcd(rows, 2)
-    back = lax.all_to_all(
-        back.reshape(HEADS, 3 * rows // pair, pair, D_HEAD),
-        AXES,
-        split_axis=0,
-        concat_axis=0,
-        tiled=True,
-    )
+    back = exchange(back.reshape(HEADS, 3 * rows // pair, pair, D_HEAD))
     out = jax.ShapeDtypeStruct(queries.shape, jnp.bfloat16)
     return pl.pallas_call(
         unpack_kernel,

time: 30.2 us -> 29.5 us (0.977)
  blocking collectives: 26.8 us -> 25.8 us
    all_to_all x2, blocking collectives: 26.8 us -> 25.8 us  [exchange(): lax.all_to_all(chunks, AXES, split_axis=0, concat_axis=0, tiled=True, axi...]
where the time goes in v3:
time: 29.5 us; the launch traced here: 28.9 us
  blocking collectives  25.8 us (87%)
  Pallas kernels  2.44 us (8%)
  between operations  0.65 us (2%)
    all_to_all x2, blocking collectives, exchange(): lax.all_to_all(chunks, AXES, split_axis=0, concat_axis=0, tiled=True, axi...  25.8 us
    pallas_call x1, Pallas kernels, by_head(): pl.pallas_call(pack_kernel, out_shape=jax.ShapeDtypeStruct((HEADS, 4 * ro...  1.02 us
    pallas_call x1, Pallas kernels, by_head(): pl.pallas_call(unpack_kernel, out_shape=(out,) * 3, in_specs=[VMEM], out_...  0.71 us
    pallas_call x1, Pallas kernels, by_head(): pl.pallas_call(lambda *refs: head_kernel(rows, *refs), out_shape=grads, i...  0.71 us

profile of v3, /device:TPU:1, one launch (start us, length us, event | category | flops | bytes accessed | tf_op | source)
XLA Modules:
  0.0 28.9 jit_solution(9131133770364613681)
XLA Ops:
  0.6 1.0 %shard_map.67 = bf16[32,24,128]{2,1,0:T(8,128)(2,1)S(1)} custom-call(bf16[6,4096]{1,0:T(8,128)(2,1)} %query_ref.1, bf16[6,4096]{1,0:T(8,128)(2,1)} %key_ref.1, bf16[6,4096]{1,0:T(8,128)(2,1)} %value_ref.1, bf16[6,4096]{1,0:T(8,128)(2,1)} %grad_ref.1), custom_call_target="tpu_custom_call" | custom-call | tf_op jit(solution)/shard_map/pallas_call | solution.py:101
  1.7 15.9 %all_to_all.10.refs_0_ = bf16[32,24,128]{2,1,0:T(8,128)(2,1)S(1)} all-to-all(bf16[32,24,128]{2,1,0:T(8,128)(2,1)S(1)} %shard_map.67), channel_id=1, replica_groups={{0,8,16,24,2,10,18,26,1,9,17,25,3,11,19,27,4,12,20,28,6,14,22,30,5,13,2..., dimensions={0} | all-to-all | bytes 393216 | tf_op jit(solution)/shard_map/all_to_all | solution.py:94
  17.6 0.7 %shard_map.68 = bf16[576,128]{1,0:T(8,128)(2,1)S(1)} custom-call(bf16[32,24,128]{2,1,0:T(8,128)(2,1)S(1)} %all_to_all.10.refs_0_), custom_call_target="tpu_custom_call" | custom-call | tf_op jit(solution)/shard_map/pallas_call | solution.py:119
  18.3 9.9 %all_to_all.11 = bf16[32,9,2,128]{3,2,1,0:T(2,128)(2,1)S(1)} all-to-all(bf16[32,9,2,128]{3,2,1,0:T(2,128)(2,1)S(1)} %bitcast.3), channel_id=1, replica_groups={{0,8,16,24,2,10,18,26,1,9,17,25,3,11,19,27,4,12,20,28,6,14,22,30,5,13,2..., dimensions={0} | all-to-all | bytes 294912 | tf_op jit(solution)/shard_map/all_to_all | solution.py:94
  28.2 0.7 %shard_map.69 = (bf16[6,4096]{1,0:T(8,128)(2,1)}, bf16[6,4096]{1,0:T(8,128)(2,1)}, bf16[6,4096]{1,0:T(8,128)(2,1)}) custom-call(bf16[576,128]{1,0:T(8,128)(2,1)S(1)} %bitcast.2), custom_call_target="tpu_custom_call" | custom-call | tf_op jit(solution)/shard_map/pallas_call | solution.py:129

commit v4 on v3

--- a/solution.py
+++ b/solution.py
@@ -1,3 +1,4 @@
+import functools
 import math
 
 import jax
@@ -10,6 +11,8 @@
 
 HEADS = 32
 D_HEAD = 128
+TILE = 8
+CORES = 2
 AXES = ("blk", "ulysses")
 HBM = pl.BlockSpec(memory_space=pltpu.HBM)
 VMEM = pl.BlockSpec(memory_space=pltpu.VMEM)
@@ -25,9 +28,13 @@
         copy.start()
     for copy in copies:
         copy.wait()
+    third = query_ref.shape[0] // 3
     for head in range(out_ref.shape[0]):
         columns = slice(head * D_HEAD, (head + 1) * D_HEAD)
-        parts = [held[which, :, columns].astype(jnp.float32) for which in range(4)]
+        *tops, grad = (held[which, :, columns].astype(jnp.float32) for which in range(4))
+        parts = []
+        for which, top in enumerate(tops):
+            parts += [top, grad[which * third : (which + 1) * third]]
         out_ref[head] = jnp.concatenate(parts, axis=0).astype(jnp.bfloat16)
 
 
@@ -37,67 +44,94 @@
     )
 
 
-def head_kernel(rows, in_ref, out_ref):
-    senders = in_ref.shape[0]
+def head_kernel(rows, places, own_ref, other_ref, out_ref):
+    senders = own_ref.shape[0]
+    heads = own_ref.shape[1] // (3 * TILE)
+    third = rows // 3
+    half = senders * TILE
     score_scale = 1.0 / math.sqrt(D_HEAD)
-    blocks = [in_ref[sender].astype(jnp.float32) for sender in range(senders)]
-
-    def gathered(which):
-        return jnp.concatenate(
-            [block[which * rows : (which + 1) * rows] for block in blocks], axis=0
-        ).astype(jnp.bfloat16)
-
-    query, key, value, grad = (gathered(which) for which in range(4))
-    logits = dot(query, key, 1, 1) * score_scale
-    top = jnp.max(logits, axis=1, keepdims=True)
-    terms = jnp.exp(logits - top)
-    weights = terms / jnp.sum(terms, axis=1, keepdims=True)
-    grad_weights = dot(grad, value, 1, 1)
-    row_dot = jnp.sum(weights * grad_weights, axis=1, keepdims=True)
-    grad_low = (weights * (grad_weights - row_dot)).astype(jnp.bfloat16)
-    weights_low = weights.astype(jnp.bfloat16)
-    grads = (
-        dot(grad_low, key, 1, 0) * score_scale,
-        dot(grad_low, query, 0, 0) * score_scale,
-        dot(weights_low, grad, 0, 0),
-    )
+    blocks = [
+        ref[sender].astype(jnp.float32)
+        for ref in (own_ref, other_ref)
+        for sender in range(senders)
+    ]
+    row = lax.broadcasted_iota(jnp.int32, (TILE, D_HEAD), 0)
+    is_key = lax.broadcasted_iota(jnp.int32, (2 * half, 2 * half), 0) % TILE < rows
+    grads = []
+    for head in range(heads):
+        tiles = [[], [], [], []]
+        for block in blocks:
+            grad = jnp.zeros((TILE, D_HEAD), jnp.float32)
+            for which in range(3):
+                first = (3 * head + which) * TILE
+                tile = block[first : first + TILE]
+                tiles[which].append(tile)
+                moved = pltpu.roll(tile, (which * third - rows) % TILE, 0)
+                inside = (row >= which * third) & (row < (which + 1) * third)
+                grad = jnp.where(inside, moved, grad)
+            tiles[3].append(grad)
+        query, key, value, grad = (
+            jnp.concatenate(parts, axis=0).astype(jnp.bfloat16) for parts in tiles
+        )
+        logits = jnp.where(is_key, dot(key, query, 1, 1), -jnp.inf)
+        grad_weights = dot(value, grad, 1, 1)
+        top = jnp.max(logits, axis=0, keepdims=True)
+        terms = jnp.exp((logits - top) * score_scale)
+        inverse = 1.0 / jnp.sum(terms, axis=0, keepdims=True)
+        row_dot = jnp.sum(terms * grad_weights, axis=0, keepdims=True) * inverse
+        weights = terms * inverse
+        grad_low = (weights * (grad_weights - row_dot)).astype(jnp.bfloat16)
+        weights_low = weights.astype(jnp.bfloat16)
+        grads += [
+            dot(grad_low[:, :half], key, 0, 0) * score_scale,
+            dot(grad_low[:half], query, 1, 0) * score_scale,
+            dot(weights_low[:half], grad, 1, 0),
+        ]
     out_ref[...] = jnp.concatenate(
         [
-            total[sender * rows : (sender + 1) * rows]
-            for sender in range(senders)
+            total[sender * TILE : sender * TILE + rows]
+            for sender in places
             for total in grads
         ],
         axis=0,
     ).astype(jnp.bfloat16)
 
 
-def unpack_kernel(in_ref, query_ref, key_ref, value_ref):
+def unpack_kernel(places, in_ref, query_ref, key_ref, value_ref):
     rows = query_ref.shape[0]
     heads = in_ref.shape[0] // (3 * rows)
     received = in_ref[...].astype(jnp.float32)
     for which, ref in enumerate((query_ref, key_ref, value_ref)):
-        for head in range(heads):
-            first = (3 * head + which) * rows
+        for place in range(heads):
+            first = (3 * place + which) * rows
+            head = CORES * places[place // CORES] + place % CORES
             columns = slice(head * D_HEAD, (head + 1) * D_HEAD)
             ref[:, columns] = received[first : first + rows].astype(jnp.bfloat16)
 
 
-def places():
-    blk_size, ulysses_size = lax.axis_size("blk"), lax.axis_size("ulysses")
-    index = np.arange(blk_size * ulysses_size)
-    if blk_size % 2 == 0 and ulysses_size % 2 == 0:
-        index = index.reshape(blk_size // 2, 2, ulysses_size // 2, 2).transpose(1, 3, 2, 0)
-    return [[int(device) for device in index.reshape(-1)]]
-
-
-def exchange(chunks):
+def chip_orders():
+    chips = HEADS // CORES
+    first = 11 * chips // 16
+    inward = [first] + [chip for chip in reversed(range(chips)) if chip != first]
+    columns = [int(chip) for chip in np.arange(chips).reshape(-1, 4).T.reshape(-1)]
+    turn = columns.index(first)
+    return inward, columns[turn:] + columns[:turn]
+
+
+def exchange(chunks, order):
+    groups = [[CORES * chip + core for chip in order] for core in range(CORES)]
     return lax.all_to_all(
-        chunks, AXES, split_axis=0, concat_axis=0, tiled=True, axis_index_groups=places()
+        chunks, AXES, split_axis=0, concat_axis=0, tiled=True, axis_index_groups=groups
     )
 
 
 def by_head(queries, key_vectors, value_vectors, cotangent):
     rows = queries.shape[0]
+    if 4 * rows != 3 * TILE:
+        return by_block(queries, key_vectors, value_vectors, cotangent)
+    chips = HEADS // CORES
+    inward, outward = chip_orders()
+    places = [inward.index(chip) for chip in outward]
     packed = pl.pallas_call(
         pack_kernel,
         out_shape=jax.ShapeDtypeStruct((HEADS, 4 * rows, D_HEAD), jnp.bfloat16),
@@ -114,20 +148,20 @@
             for array in (queries, key_vectors, value_vectors, cotangent)
         )
     )
-    held = exchange(packed)
+    own = exchange(packed.reshape(chips, CORES * 4 * rows, D_HEAD), inward)
+    other = lax.ppermute(own, AXES, [(device, device ^ 1) for device in range(HEADS)])
     grads = jax.ShapeDtypeStruct((HEADS * 3 * rows, D_HEAD), jnp.bfloat16)
     back = pl.pallas_call(
-        lambda *refs: head_kernel(rows, *refs),
+        functools.partial(head_kernel, rows, places),
         out_shape=grads,
-        in_specs=[VMEM],
+        in_specs=[VMEM] * 2,
         out_specs=VMEM,
         compiler_params=PARAMS,
-    )(held)
-    pair = math.gcd(rows, 2)
-    back = exchange(back.reshape(HEADS, 3 * rows // pair, pair, D_HEAD))
+    )(own, other)
+    back = exchange(back.reshape(chips, CORES * 3 * rows // 2, 2, D_HEAD), outward)
     out = jax.ShapeDtypeStruct(queries.shape, jnp.bfloat16)
     return pl.pallas_call(
-        unpack_kernel,
+        functools.partial(unpack_kernel, places),
         out_shape=(out,) * 3,
         in_specs=[VMEM],
         out_specs=(VMEM,) * 3,
@@ -228,7 +262,8 @@
         P(("blk", "ulysses"), None),
         P(("blk", "ulysses"), None),
     )
-    local = by_head if mesh.size == HEADS else by_block
+    by_heads = mesh.size == HEADS and mesh.shape["ulysses"] % CORES == 0
+    local = by_head if by_heads else by_block
     return jax.shard_map(
         local,
         mesh=mesh,

time: 29.5 us -> 28.8 us (0.976)
  the two profiles are of different devices: /device:TPU:1 before, /device:TPU:0 now
where the time goes in v4:
time: 28.8 us; the launch traced here: 28.5 us
  blocking collectives  23.8 us (83%)
  Pallas kernels  2.62 us (9%)
  waiting for transfers between devices  1.44 us (5%)
  between operations  0.65 us (2%)
    all_to_all x2, blocking collectives, exchange(): lax.all_to_all(chunks, AXES, split_axis=0, concat_axis=0, tiled=True, axi...  23.8 us
    ppermute x1, waiting for transfers between devices, by_head(): lax.ppermute(own, AXES, [(device, device ^ 1) for device in range(HEADS)])  1.44 us
    pallas_call x1, Pallas kernels, by_head(): pl.pallas_call(pack_kernel, out_shape=jax.ShapeDtypeStruct((HEADS, 4 * ro...  1.02 us
    pallas_call x1, Pallas kernels, by_head(): pl.pallas_call(functools.partial(head_kernel, rows, places), out_shape=gr...  0.88 us
    pallas_call x1, Pallas kernels, by_head(): pl.pallas_call(functools.partial(unpack_kernel, places), out_shape=(out,)...  0.71 us
  transfers between devices with their start and end apart: 1, of which 1 were waited for; matrix products, arithmetic and copies ran while one was open for 0% of the time, Pallas kernels for 0%

profile of v4, /device:TPU:0, one launch (start us, length us, event | category | flops | bytes accessed | tf_op | source)
XLA Modules:
  0.0 28.5 jit_solution(14509238005606103722)
XLA Ops:
  0.6 1.0 %shard_map.67 = bf16[32,24,128]{2,1,0:T(8,128)(2,1)S(1)} custom-call(bf16[6,4096]{1,0:T(8,128)(2,1)} %query_ref.1, bf16[6,4096]{1,0:T(8,128)(2,1)} %key_ref.1, bf16[6,4096]{1,0:T(8,128)(2,1)} %value_ref.1, bf16[6,4096]{1,0:T(8,128)(2,1)} %grad_ref.1), custom_call_target="tpu_custom_call" | custom-call | tf_op jit(solution)/shard_map/pallas_call | solution.py:135
  1.7 13.7 %all_to_all.10.own_ref = bf16[16,48,128]{2,1,0:T(8,128)(2,1)S(1)} all-to-all(bf16[16,48,128]{2,1,0:T(8,128)(2,1)S(1)} %bitcast.3), channel_id=1, replica_groups={{22,30,28,26,24,20,18,16,14,12,10,8,6,4,2,0},{23,31,29,27,25,21,19,17,1..., dimensions={0} | all-to-all | bytes 393216 | tf_op jit(solution)/shard_map/all_to_all | solution.py:123
  15.4 0.0 collective-permute-start
  15.4 1.4 %collective-permute-done.other_ref = bf16[16,48,128]{2,1,0:T(8,128)(2,1)S(1)} collective-permute-done((bf16[16,48,128]{2,1,0:T(8,128)(2,1)S(1)}, bf16[16,48,128]{2,1,0:T(8,128)(2,1)S(1)}, u32[]{:S(2)}, u32[]{:S(2)}) %collective-permute-start) | collective-permute-done | bytes 196640 | tf_op jit(solution)/shard_map/ppermute | solution.py:152
  16.8 0.9 %shard_map.68 = bf16[576,128]{1,0:T(8,128)(2,1)S(1)} custom-call(bf16[16,48,128]{2,1,0:T(8,128)(2,1)S(1)} %all_to_all.10.own_ref, bf16[16,48,128]{2,1,0:T(8,128)(2,1)S(1)} %collective-permute-done.other_ref), custom_call_target="tpu_custom_call" | custom-call | tf_op jit(solution)/shard_map/pallas_call | solution.py:154
  17.7 10.1 %all_to_all.11 = bf16[16,18,2,128]{3,2,1,0:T(2,128)(2,1)S(1)} all-to-all(bf16[16,18,2,128]{3,2,1,0:T(2,128)(2,1)S(1)} %bitcast.5), channel_id=1, replica_groups={{22,30,0,8,16,24,2,10,18,26,4,12,20,28,6,14},{23,31,1,9,17,25,3,11,19,2..., dimensions={0} | all-to-all | bytes 294912 | tf_op jit(solution)/shard_map/all_to_all | solution.py:123
  27.8 0.7 %shard_map.69 = (bf16[6,4096]{1,0:T(8,128)(2,1)}, bf16[6,4096]{1,0:T(8,128)(2,1)}, bf16[6,4096]{1,0:T(8,128)(2,1)}) custom-call(bf16[576,128]{1,0:T(8,128)(2,1)S(1)} %bitcast.4), custom_call_target="tpu_custom_call" | custom-call | tf_op jit(solution)/shard_map/pallas_call | solution.py:163
Async XLA Ops:
  15.4 1.4 %collective-permute-start = (bf16[16,48,128]{2,1,0:T(8,128)(2,1)S(1)}, bf16[16,48,128]{2,1,0:T(8,128)(2,1)S(1)}, u32[]{:S(2)}, u32[]{:S(2)}) collective-permute-start(bf16[16,48,128]{2,1,0:T(8,128)(2,1)S(1)} %all_to_all.10.own_ref), channel_id=1, source_target_pairs={{0,1},{1,0},{2,3},{3,2},{4,5},{5,4},{6,7},{7,6},{8,9},{9,8},{10,11... | collective-permute-start | bytes 589832 | tf_op jit(solution)/shard_map/ppermute | solution.py:152

commit v5 on v4

--- a/solution.py
+++ b/solution.py
@@ -14,6 +14,9 @@
 TILE = 8
 CORES = 2
 AXES = ("blk", "ulysses")
+INWARD = (11, 10, 9, 12, 5, 7, 4, 6, 3, 2, 1, 0, 15, 8, 13, 14)
+OUTWARD = (11, 15, 0, 4, 14, 10, 2, 6, 13, 9, 5, 1, 12, 8, 3, 7)
+TURNED = (0, 1)
 HBM = pl.BlockSpec(memory_space=pltpu.HBM)
 VMEM = pl.BlockSpec(memory_space=pltpu.VMEM)
 PARAMS = pltpu.CompilerParams(vmem_limit_bytes=8 * 2**20)
@@ -109,17 +112,10 @@
             ref[:, columns] = received[first : first + rows].astype(jnp.bfloat16)
 
 
-def chip_orders():
-    chips = HEADS // CORES
-    first = 11 * chips // 16
-    inward = [first] + [chip for chip in reversed(range(chips)) if chip != first]
-    columns = [int(chip) for chip in np.arange(chips).reshape(-1, 4).T.reshape(-1)]
-    turn = columns.index(first)
-    return inward, columns[turn:] + columns[:turn]
-
-
 def exchange(chunks, order):
-    groups = [[CORES * chip + core for chip in order] for core in range(CORES)]
+    groups = [
+        [CORES * chip + (core ^ (chip in TURNED)) for chip in order] for core in range(CORES)
+    ]
     return lax.all_to_all(
         chunks, AXES, split_axis=0, concat_axis=0, tiled=True, axis_index_groups=groups
     )
@@ -130,8 +126,7 @@
     if 4 * rows != 3 * TILE:
         return by_block(queries, key_vectors, value_vectors, cotangent)
     chips = HEADS // CORES
-    inward, outward = chip_orders()
-    places = [inward.index(chip) for chip in outward]
+    places = [INWARD.index(chip) for chip in OUTWARD]
     packed = pl.pallas_call(
         pack_kernel,
         out_shape=jax.ShapeDtypeStruct((HEADS, 4 * rows, D_HEAD), jnp.bfloat16),
@@ -148,7 +143,7 @@
             for array in (queries, key_vectors, value_vectors, cotangent)
         )
     )
-    own = exchange(packed.reshape(chips, CORES * 4 * rows, D_HEAD), inward)
+    own = exchange(packed.reshape(chips, CORES * 4 * rows, D_HEAD), INWARD)
     other = lax.ppermute(own, AXES, [(device, device ^ 1) for device in range(HEADS)])
     grads = jax.ShapeDtypeStruct((HEADS * 3 * rows, D_HEAD), jnp.bfloat16)
     back = pl.pallas_call(
@@ -158,7 +153,7 @@
         out_specs=VMEM,
         compiler_params=PARAMS,
     )(own, other)
-    back = exchange(back.reshape(chips, CORES * 3 * rows // 2, 2, D_HEAD), outward)
+    back = exchange(back.reshape(chips, CORES * 3 * rows // 2, 2, D_HEAD), OUTWARD)
     out = jax.ShapeDtypeStruct(queries.shape, jnp.bfloat16)
     return pl.pallas_call(
         functools.partial(unpack_kernel, places),
@@ -262,7 +257,7 @@
         P(("blk", "ulysses"), None),
         P(("blk", "ulysses"), None),
     )
-    by_heads = mesh.size == HEADS and mesh.shape["ulysses"] % CORES == 0
+    by_heads = mesh.size == HEADS == CORES * len(INWARD) and mesh.shape["ulysses"] % CORES == 0
     local = by_head if by_heads else by_block
     return jax.shard_map(
         local,

time: 28.8 us -> 28 us (0.972)
  the two profiles are of different devices: /device:TPU:0 before, /device:TPU:1 now
where the time goes in v5:
time: 28 us; the launch traced here: 27.8 us
  blocking collectives  23.1 us (82%)
  Pallas kernels  2.62 us (9%)
  waiting for transfers between devices  1.44 us (5%)
  between operations  0.65 us (2%)
    all_to_all x2, blocking collectives, exchange(): lax.all_to_all(chunks, AXES, split_axis=0, concat_axis=0, tiled=True, axi...  23.1 us
    ppermute x1, waiting for transfers between devices, by_head(): lax.ppermute(own, AXES, [(device, device ^ 1) for device in range(HEADS)])  1.44 us
    pallas_call x1, Pallas kernels, by_head(): pl.pallas_call(pack_kernel, out_shape=jax.ShapeDtypeStruct((HEADS, 4 * ro...  1.02 us
    pallas_call x1, Pallas kernels, by_head(): pl.pallas_call(functools.partial(head_kernel, rows, places), out_shape=gr...  0.88 us
    pallas_call x1, Pallas kernels, by_head(): pl.pallas_call(functools.partial(unpack_kernel, places), out_shape=(out,)...  0.71 us
  transfers between devices with their start and end apart: 1, of which 1 were waited for; matrix products, arithmetic and copies ran while one was open for 0% of the time, Pallas kernels for 0%

profile of v5, /device:TPU:1, one launch (start us, length us, event | category | flops | bytes accessed | tf_op | source)
XLA Modules:
  0.0 27.8 jit_solution(11801514861220754572)
XLA Ops:
  0.6 1.0 %shard_map.67 = bf16[32,24,128]{2,1,0:T(8,128)(2,1)S(1)} custom-call(bf16[6,4096]{1,0:T(8,128)(2,1)} %query_ref.1, bf16[6,4096]{1,0:T(8,128)(2,1)} %key_ref.1, bf16[6,4096]{1,0:T(8,128)(2,1)} %value_ref.1, bf16[6,4096]{1,0:T(8,128)(2,1)} %grad_ref.1), custom_call_target="tpu_custom_call" | custom-call | tf_op jit(solution)/shard_map/pallas_call | solution.py:130
  1.7 13.0 %all_to_all.10.own_ref = bf16[16,48,128]{2,1,0:T(8,128)(2,1)S(1)} all-to-all(bf16[16,48,128]{2,1,0:T(8,128)(2,1)S(1)} %bitcast.3), channel_id=1, replica_groups={{22,20,18,24,10,14,8,12,6,4,3,1,30,16,26,28},{23,21,19,25,11,15,9,13,7,..., dimensions={0} | all-to-all | bytes 393216 | tf_op jit(solution)/shard_map/all_to_all | solution.py:119
  14.7 0.0 collective-permute-start
  14.7 1.4 %collective-permute-done.other_ref = bf16[16,48,128]{2,1,0:T(8,128)(2,1)S(1)} collective-permute-done((bf16[16,48,128]{2,1,0:T(8,128)(2,1)S(1)}, bf16[16,48,128]{2,1,0:T(8,128)(2,1)S(1)}, u32[]{:S(2)}, u32[]{:S(2)}) %collective-permute-start) | collective-permute-done | bytes 196640 | tf_op jit(solution)/shard_map/ppermute | solution.py:147
  16.1 0.9 %shard_map.68 = bf16[576,128]{1,0:T(8,128)(2,1)S(1)} custom-call(bf16[16,48,128]{2,1,0:T(8,128)(2,1)S(1)} %all_to_all.10.own_ref, bf16[16,48,128]{2,1,0:T(8,128)(2,1)S(1)} %collective-permute-done.other_ref), custom_call_target="tpu_custom_call" | custom-call | tf_op jit(solution)/shard_map/pallas_call | solution.py:149
  17.0 10.0 %all_to_all.11 = bf16[16,18,2,128]{3,2,1,0:T(2,128)(2,1)S(1)} all-to-all(bf16[16,18,2,128]{3,2,1,0:T(2,128)(2,1)S(1)} %bitcast.5), channel_id=1, replica_groups={{22,30,1,8,28,20,4,12,26,18,10,3,24,16,6,14},{23,31,0,9,29,21,5,13,27,1..., dimensions={0} | all-to-all | bytes 294912 | tf_op jit(solution)/shard_map/all_to_all | solution.py:119
  27.1 0.7 %shard_map.69 = (bf16[6,4096]{1,0:T(8,128)(2,1)}, bf16[6,4096]{1,0:T(8,128)(2,1)}, bf16[6,4096]{1,0:T(8,128)(2,1)}) custom-call(bf16[576,128]{1,0:T(8,128)(2,1)S(1)} %bitcast.4), custom_call_target="tpu_custom_call" | custom-call | tf_op jit(solution)/shard_map/pallas_call | solution.py:158
Async XLA Ops:
  14.7 1.4 %collective-permute-start = (bf16[16,48,128]{2,1,0:T(8,128)(2,1)S(1)}, bf16[16,48,128]{2,1,0:T(8,128)(2,1)S(1)}, u32[]{:S(2)}, u32[]{:S(2)}) collective-permute-start(bf16[16,48,128]{2,1,0:T(8,128)(2,1)S(1)} %all_to_all.10.own_ref), channel_id=1, source_target_pairs={{0,1},{1,0},{2,3},{3,2},{4,5},{5,4},{6,7},{7,6},{8,9},{9,8},{10,11... | collective-permute-start | bytes 589832 | tf_op jit(solution)/shard_map/ppermute | solution.py:147

commit v6 on v5

--- a/solution.py
+++ b/solution.py
@@ -3,7 +3,6 @@
 
 import jax
 import jax.numpy as jnp
-import numpy as np
 from jax import lax
 from jax.experimental import pallas as pl
 from jax.experimental.pallas import tpu as pltpu
@@ -14,8 +13,8 @@
 TILE = 8
 CORES = 2
 AXES = ("blk", "ulysses")
-INWARD = (11, 10, 9, 12, 5, 7, 4, 6, 3, 2, 1, 0, 15, 8, 13, 14)
-OUTWARD = (11, 15, 0, 4, 14, 10, 2, 6, 13, 9, 5, 1, 12, 8, 3, 7)
+INWARD = (11, 10, 9, 5, 7, 4, 6, 3, 2, 1, 0, 15, 8, 12, 13, 14)
+OUTWARD = (11, 15, 0, 4, 14, 9, 2, 6, 13, 10, 3, 1, 12, 8, 5, 7)
 TURNED = (0, 1)
 HBM = pl.BlockSpec(memory_space=pltpu.HBM)
 VMEM = pl.BlockSpec(memory_space=pltpu.VMEM)

time: 28 us -> 27.9 us (level)
  no operation moved by 1% of the time
where the time goes in v6:
time: 27.9 us; the launch traced here: 27.7 us
  blocking collectives  23 us (82%)
  Pallas kernels  2.62 us (9%)
  waiting for transfers between devices  1.44 us (5%)
  between operations  0.65 us (2%)
    all_to_all x2, blocking collectives, exchange(): lax.all_to_all(chunks, AXES, split_axis=0, concat_axis=0, tiled=True, axi...  23 us
    ppermute x1, waiting for transfers between devices, by_head(): lax.ppermute(own, AXES, [(device, device ^ 1) for device in range(HEADS)])  1.44 us
    pallas_call x1, Pallas kernels, by_head(): pl.pallas_call(pack_kernel, out_shape=jax.ShapeDtypeStruct((HEADS, 4 * ro...  1.02 us
    pallas_call x1, Pallas kernels, by_head(): pl.pallas_call(functools.partial(head_kernel, rows, places), out_shape=gr...  0.89 us
    pallas_call x1, Pallas kernels, by_head(): pl.pallas_call(functools.partial(unpack_kernel, places), out_shape=(out,)...  0.71 us
  transfers between devices with their start and end apart: 1, of which 1 were waited for; matrix products, arithmetic and copies ran while one was open for 0% of the time, Pallas kernels for 0%

profile of v6, /device:TPU:1, one launch (start us, length us, event | category | flops | bytes accessed | tf_op | source)
XLA Modules:
  0.0 27.7 jit_solution(8722346320211739122)
XLA Ops:
  0.6 1.0 %shard_map.67 = bf16[32,24,128]{2,1,0:T(8,128)(2,1)S(1)} custom-call(bf16[6,4096]{1,0:T(8,128)(2,1)} %query_ref.1, bf16[6,4096]{1,0:T(8,128)(2,1)} %key_ref.1, bf16[6,4096]{1,0:T(8,128)(2,1)} %value_ref.1, bf16[6,4096]{1,0:T(8,128)(2,1)} %grad_ref.1), custom_call_target="tpu_custom_call" | custom-call | tf_op jit(solution)/shard_map/pallas_call | solution.py:129
  1.7 13.1 %all_to_all.10.own_ref = bf16[16,48,128]{2,1,0:T(8,128)(2,1)S(1)} all-to-all(bf16[16,48,128]{2,1,0:T(8,128)(2,1)S(1)} %bitcast.3), channel_id=1, replica_groups={{22,20,18,10,14,8,12,6,4,3,1,30,16,24,26,28},{23,21,19,11,15,9,13,7,5,2..., dimensions={0} | all-to-all | bytes 393216 | tf_op jit(solution)/shard_map/all_to_all | solution.py:118
  14.7 0.0 collective-permute-start
  14.7 1.4 %collective-permute-done.other_ref = bf16[16,48,128]{2,1,0:T(8,128)(2,1)S(1)} collective-permute-done((bf16[16,48,128]{2,1,0:T(8,128)(2,1)S(1)}, bf16[16,48,128]{2,1,0:T(8,128)(2,1)S(1)}, u32[]{:S(2)}, u32[]{:S(2)}) %collective-permute-start) | collective-permute-done | bytes 196640 | tf_op jit(solution)/shard_map/ppermute | solution.py:146
  16.2 0.9 %shard_map.68 = bf16[576,128]{1,0:T(8,128)(2,1)S(1)} custom-call(bf16[16,48,128]{2,1,0:T(8,128)(2,1)S(1)} %all_to_all.10.own_ref, bf16[16,48,128]{2,1,0:T(8,128)(2,1)S(1)} %collective-permute-done.other_ref), custom_call_target="tpu_custom_call" | custom-call | tf_op jit(solution)/shard_map/pallas_call | solution.py:148
  17.1 9.9 %all_to_all.11 = bf16[16,18,2,128]{3,2,1,0:T(2,128)(2,1)S(1)} all-to-all(bf16[16,18,2,128]{3,2,1,0:T(2,128)(2,1)S(1)} %bitcast.5), channel_id=1, replica_groups={{22,30,1,8,28,18,4,12,26,20,6,3,24,16,10,14},{23,31,0,9,29,19,5,13,27,2..., dimensions={0} | all-to-all | bytes 294912 | tf_op jit(solution)/shard_map/all_to_all | solution.py:118
  27.0 0.7 %shard_map.69 = (bf16[6,4096]{1,0:T(8,128)(2,1)}, bf16[6,4096]{1,0:T(8,128)(2,1)}, bf16[6,4096]{1,0:T(8,128)(2,1)}) custom-call(bf16[576,128]{1,0:T(8,128)(2,1)S(1)} %bitcast.4), custom_call_target="tpu_custom_call" | custom-call | tf_op jit(solution)/shard_map/pallas_call | solution.py:157
Async XLA Ops:
  14.7 1.4 %collective-permute-start = (bf16[16,48,128]{2,1,0:T(8,128)(2,1)S(1)}, bf16[16,48,128]{2,1,0:T(8,128)(2,1)S(1)}, u32[]{:S(2)}, u32[]{:S(2)}) collective-permute-start(bf16[16,48,128]{2,1,0:T(8,128)(2,1)S(1)} %all_to_all.10.own_ref), channel_id=1, source_target_pairs={{0,1},{1,0},{2,3},{3,2},{4,5},{5,4},{6,7},{7,6},{8,9},{9,8},{10,11... | collective-permute-start | bytes 589832 | tf_op jit(solution)/shard_map/ppermute | solution.py:146

commit v7 on v6

--- a/solution.py
+++ b/solution.py
@@ -14,7 +14,7 @@
 CORES = 2
 AXES = ("blk", "ulysses")
 INWARD = (11, 10, 9, 5, 7, 4, 6, 3, 2, 1, 0, 15, 8, 12, 13, 14)
-OUTWARD = (11, 15, 0, 4, 14, 9, 2, 6, 13, 10, 3, 1, 12, 8, 5, 7)
+OUTWARD = (11, 15, 0, 4, 14, 7, 5, 8, 12, 2, 3, 10, 13, 6, 1, 9)
 TURNED = (0, 1)
 HBM = pl.BlockSpec(memory_space=pltpu.HBM)
 VMEM = pl.BlockSpec(memory_space=pltpu.VMEM)

time: 27.9 us -> 27.9 us (level)
  no operation moved by 1% of the time
where the time goes in v7:
time: 27.9 us; the launch traced here: 27.6 us
  blocking collectives  22.9 us (82%)
  Pallas kernels  2.62 us (9%)
  waiting for transfers between devices  1.44 us (5%)
  between operations  0.65 us (2%)
    all_to_all x2, blocking collectives, exchange(): lax.all_to_all(chunks, AXES, split_axis=0, concat_axis=0, tiled=True, axi...  22.9 us
    ppermute x1, waiting for transfers between devices, by_head(): lax.ppermute(own, AXES, [(device, device ^ 1) for device in range(HEADS)])  1.44 us
    pallas_call x1, Pallas kernels, by_head(): pl.pallas_call(pack_kernel, out_shape=jax.ShapeDtypeStruct((HEADS, 4 * ro...  1.02 us
    pallas_call x1, Pallas kernels, by_head(): pl.pallas_call(functools.partial(head_kernel, rows, places), out_shape=gr...  0.89 us
    pallas_call x1, Pallas kernels, by_head(): pl.pallas_call(functools.partial(unpack_kernel, places), out_shape=(out,)...  0.71 us
  transfers between devices with their start and end apart: 1, of which 1 were waited for; matrix products, arithmetic and copies ran while one was open for 0% of the time, Pallas kernels for 0%

profile of v7, /device:TPU:1, one launch (start us, length us, event | category | flops | bytes accessed | tf_op | source)
XLA Modules:
  0.0 27.6 jit_solution(8598358129288135551)
XLA Ops:
  0.6 1.0 %shard_map.67 = bf16[32,24,128]{2,1,0:T(8,128)(2,1)S(1)} custom-call(bf16[6,4096]{1,0:T(8,128)(2,1)} %query_ref.1, bf16[6,4096]{1,0:T(8,128)(2,1)} %key_ref.1, bf16[6,4096]{1,0:T(8,128)(2,1)} %value_ref.1, bf16[6,4096]{1,0:T(8,128)(2,1)} %grad_ref.1), custom_call_target="tpu_custom_call" | custom-call | tf_op jit(solution)/shard_map/pallas_call | solution.py:129
  1.7 13.1 %all_to_all.10.own_ref = bf16[16,48,128]{2,1,0:T(8,128)(2,1)S(1)} all-to-all(bf16[16,48,128]{2,1,0:T(8,128)(2,1)S(1)} %bitcast.3), channel_id=1, replica_groups={{22,20,18,10,14,8,12,6,4,3,1,30,16,24,26,28},{23,21,19,11,15,9,13,7,5,2..., dimensions={0} | all-to-all | bytes 393216 | tf_op jit(solution)/shard_map/all_to_all | solution.py:118
  14.7 0.0 collective-permute-start
  14.7 1.4 %collective-permute-done.other_ref = bf16[16,48,128]{2,1,0:T(8,128)(2,1)S(1)} collective-permute-done((bf16[16,48,128]{2,1,0:T(8,128)(2,1)S(1)}, bf16[16,48,128]{2,1,0:T(8,128)(2,1)S(1)}, u32[]{:S(2)}, u32[]{:S(2)}) %collective-permute-start) | collective-permute-done | bytes 196640 | tf_op jit(solution)/shard_map/ppermute | solution.py:146
  16.2 0.9 %shard_map.68 = bf16[576,128]{1,0:T(8,128)(2,1)S(1)} custom-call(bf16[16,48,128]{2,1,0:T(8,128)(2,1)S(1)} %all_to_all.10.own_ref, bf16[16,48,128]{2,1,0:T(8,128)(2,1)S(1)} %collective-permute-done.other_ref), custom_call_target="tpu_custom_call" | custom-call | tf_op jit(solution)/shard_map/pallas_call | solution.py:148
  17.1 9.8 %all_to_all.11 = bf16[16,18,2,128]{3,2,1,0:T(2,128)(2,1)S(1)} all-to-all(bf16[16,18,2,128]{3,2,1,0:T(2,128)(2,1)S(1)} %bitcast.5), channel_id=1, replica_groups={{22,30,1,8,28,14,10,16,24,4,6,20,26,12,3,18},{23,31,0,9,29,15,11,17,25,..., dimensions={0} | all-to-all | bytes 294912 | tf_op jit(solution)/shard_map/all_to_all | solution.py:118
  26.9 0.7 %shard_map.69 = (bf16[6,4096]{1,0:T(8,128)(2,1)}, bf16[6,4096]{1,0:T(8,128)(2,1)}, bf16[6,4096]{1,0:T(8,128)(2,1)}) custom-call(bf16[576,128]{1,0:T(8,128)(2,1)S(1)} %bitcast.4), custom_call_target="tpu_custom_call" | custom-call | tf_op jit(solution)/shard_map/pallas_call | solution.py:157
Async XLA Ops:
  14.7 1.4 %collective-permute-start = (bf16[16,48,128]{2,1,0:T(8,128)(2,1)S(1)}, bf16[16,48,128]{2,1,0:T(8,128)(2,1)S(1)}, u32[]{:S(2)}, u32[]{:S(2)}) collective-permute-start(bf16[16,48,128]{2,1,0:T(8,128)(2,1)S(1)} %all_to_all.10.own_ref), channel_id=1, source_target_pairs={{0,1},{1,0},{2,3},{3,2},{4,5},{5,4},{6,7},{7,6},{8,9},{9,8},{10,11... | collective-permute-start | bytes 589832 | tf_op jit(solution)/shard_map/ppermute | solution.py:146

commit v8 on v7

--- a/solution.py
+++ b/solution.py
@@ -22,22 +22,30 @@
 
 
 def pack_kernel(query_ref, key_ref, value_ref, grad_ref, out_ref, held, arrived):
+    rows, columns = query_ref.shape
+    halves = [slice(part * columns // 2, (part + 1) * columns // 2) for part in range(2)]
     copies = [
-        pltpu.make_async_copy(ref, held.at[which], arrived.at[which])
-        for which, ref in enumerate((query_ref, key_ref, value_ref, grad_ref))
+        [
+            pltpu.make_async_copy(ref.at[:, half], held.at[which, :, half], arrived.at[part, which])
+            for which, ref in enumerate((query_ref, key_ref, value_ref, grad_ref))
+        ]
+        for part, half in enumerate(halves)
     ]
-    for copy in copies:
-        copy.start()
-    for copy in copies:
-        copy.wait()
-    third = query_ref.shape[0] // 3
-    for head in range(out_ref.shape[0]):
-        columns = slice(head * D_HEAD, (head + 1) * D_HEAD)
-        *tops, grad = (held[which, :, columns].astype(jnp.float32) for which in range(4))
-        parts = []
-        for which, top in enumerate(tops):
-            parts += [top, grad[which * third : (which + 1) * third]]
-        out_ref[head] = jnp.concatenate(parts, axis=0).astype(jnp.bfloat16)
+    for part in copies:
+        for copy in part:
+            copy.start()
+    third = rows // 3
+    heads = out_ref.shape[0]
+    for part in range(2):
+        for copy in copies[part]:
+            copy.wait()
+        for head in range(part * heads // 2, (part + 1) * heads // 2):
+            columns = slice(head * D_HEAD, (head + 1) * D_HEAD)
+            *tops, grad = (held[which, :, columns].astype(jnp.float32) for which in range(4))
+            parts = []
+            for which, top in enumerate(tops):
+                parts += [top, grad[which * third : (which + 1) * third]]
+            out_ref[head] = jnp.concatenate(parts, axis=0).astype(jnp.bfloat16)
 
 
 def dot(left, right, left_dim, right_dim):
@@ -61,20 +69,27 @@
     is_key = lax.broadcasted_iota(jnp.int32, (2 * half, 2 * half), 0) % TILE < rows
     grads = []
     for head in range(heads):
-        tiles = [[], [], [], []]
+        first = 3 * head * TILE
+        query, key, value = (
+            jnp.concatenate(
+                [
+                    ref[:, first + which * TILE : first + (which + 1) * TILE].reshape(half, D_HEAD)
+                    for ref in (own_ref, other_ref)
+                ],
+                axis=0,
+            )
+            for which in range(3)
+        )
+        parts = []
         for block in blocks:
             grad = jnp.zeros((TILE, D_HEAD), jnp.float32)
             for which in range(3):
-                first = (3 * head + which) * TILE
-                tile = block[first : first + TILE]
-                tiles[which].append(tile)
+                tile = block[first + which * TILE : first + (which + 1) * TILE]
                 moved = pltpu.roll(tile, (which * third - rows) % TILE, 0)
                 inside = (row >= which * third) & (row < (which + 1) * third)
                 grad = jnp.where(inside, moved, grad)
-            tiles[3].append(grad)
-        query, key, value, grad = (
-            jnp.concatenate(parts, axis=0).astype(jnp.bfloat16) for parts in tiles
-        )
+            parts.append(grad)
+        grad = jnp.concatenate(parts, axis=0).astype(jnp.bfloat16)
         logits = jnp.where(is_key, dot(key, query, 1, 1), -jnp.inf)
         grad_weights = dot(value, grad, 1, 1)
         top = jnp.max(logits, axis=0, keepdims=True)
@@ -133,7 +148,7 @@
         out_specs=VMEM,
         scratch_shapes=[
             pltpu.VMEM((4,) + queries.shape, jnp.bfloat16),
-            pltpu.SemaphoreType.DMA((4,)),
+            pltpu.SemaphoreType.DMA((2, 4)),
         ],
         compiler_params=PARAMS,
     )(

time: 27.9 us -> 27.8 us (level)
  no operation moved by 1% of the time
where the time goes in v8:
time: 27.8 us; the launch traced here: 27.6 us
  blocking collectives  22.9 us (82%)
  Pallas kernels  2.56 us (9%)
  waiting for transfers between devices  1.44 us (5%)
  between operations  0.65 us (2%)
    all_to_all x2, blocking collectives, exchange(): lax.all_to_all(chunks, AXES, split_axis=0, concat_axis=0, tiled=True, axi...  22.9 us
    ppermute x1, waiting for transfers between devices, by_head(): lax.ppermute(own, AXES, [(device, device ^ 1) for device in range(HEADS)])  1.44 us
    pallas_call x1, Pallas kernels, by_head(): pl.pallas_call(pack_kernel, out_shape=jax.ShapeDtypeStruct((HEADS, 4 * ro...  0.97 us
    pallas_call x1, Pallas kernels, by_head(): pl.pallas_call(functools.partial(head_kernel, rows, places), out_shape=gr...  0.88 us
    pallas_call x1, Pallas kernels, by_head(): pl.pallas_call(functools.partial(unpack_kernel, places), out_shape=(out,)...  0.71 us
  transfers between devices with their start and end apart: 1, of which 1 were waited for; matrix products, arithmetic and copies ran while one was open for 0% of the time, Pallas kernels for 0%

profile of v8, /device:TPU:1, one launch (start us, length us, event | category | flops | bytes accessed | tf_op | source)
XLA Modules:
  0.0 27.6 jit_solution(1183139606764761100)
XLA Ops:
  0.6 1.0 %shard_map.67 = bf16[32,24,128]{2,1,0:T(8,128)(2,1)S(1)} custom-call(bf16[6,4096]{1,0:T(8,128)(2,1)} %query_ref.1, bf16[6,4096]{1,0:T(8,128)(2,1)} %key_ref.1, bf16[6,4096]{1,0:T(8,128)(2,1)} %value_ref.1, bf16[6,4096]{1,0:T(8,128)(2,1)} %grad_ref.1), custom_call_target="tpu_custom_call" | custom-call | tf_op jit(solution)/shard_map/pallas_call | solution.py:144
  1.6 13.1 %all_to_all.10.own_ref = bf16[16,48,128]{2,1,0:T(8,128)(2,1)S(1)} all-to-all(bf16[16,48,128]{2,1,0:T(8,128)(2,1)S(1)} %bitcast.3), channel_id=1, replica_groups={{22,20,18,10,14,8,12,6,4,3,1,30,16,24,26,28},{23,21,19,11,15,9,13,7,5,2..., dimensions={0} | all-to-all | bytes 393216 | tf_op jit(solution)/shard_map/all_to_all | solution.py:133
  14.7 0.0 collective-permute-start
  14.7 1.4 %collective-permute-done.other_ref = bf16[16,48,128]{2,1,0:T(8,128)(2,1)S(1)} collective-permute-done((bf16[16,48,128]{2,1,0:T(8,128)(2,1)S(1)}, bf16[16,48,128]{2,1,0:T(8,128)(2,1)S(1)}, u32[]{:S(2)}, u32[]{:S(2)}) %collective-permute-start) | collective-permute-done | bytes 196640 | tf_op jit(solution)/shard_map/ppermute | solution.py:161
  16.1 0.9 %shard_map.68 = bf16[576,128]{1,0:T(8,128)(2,1)S(1)} custom-call(bf16[16,48,128]{2,1,0:T(8,128)(2,1)S(1)} %all_to_all.10.own_ref, bf16[16,48,128]{2,1,0:T(8,128)(2,1)S(1)} %collective-permute-done.other_ref), custom_call_target="tpu_custom_call" | custom-call | tf_op jit(solution)/shard_map/pallas_call | solution.py:163
  17.0 9.8 %all_to_all.11 = bf16[16,18,2,128]{3,2,1,0:T(2,128)(2,1)S(1)} all-to-all(bf16[16,18,2,128]{3,2,1,0:T(2,128)(2,1)S(1)} %bitcast.5), channel_id=1, replica_groups={{22,30,1,8,28,14,10,16,24,4,6,20,26,12,3,18},{23,31,0,9,29,15,11,17,25,..., dimensions={0} | all-to-all | bytes 294912 | tf_op jit(solution)/shard_map/all_to_all | solution.py:133
  26.9 0.7 %shard_map.69 = (bf16[6,4096]{1,0:T(8,128)(2,1)}, bf16[6,4096]{1,0:T(8,128)(2,1)}, bf16[6,4096]{1,0:T(8,128)(2,1)}) custom-call(bf16[576,128]{1,0:T(8,128)(2,1)S(1)} %bitcast.4), custom_call_target="tpu_custom_call" | custom-call | tf_op jit(solution)/shard_map/pallas_call | solution.py:172
Async XLA Ops:
  14.7 1.4 %collective-permute-start = (bf16[16,48,128]{2,1,0:T(8,128)(2,1)S(1)}, bf16[16,48,128]{2,1,0:T(8,128)(2,1)S(1)}, u32[]{:S(2)}, u32[]{:S(2)}) collective-permute-start(bf16[16,48,128]{2,1,0:T(8,128)(2,1)S(1)} %all_to_all.10.own_ref), channel_id=1, source_target_pairs={{0,1},{1,0},{2,3},{3,2},{4,5},{5,4},{6,7},{7,6},{8,9},{9,8},{10,11... | collective-permute-start | bytes 589832 | tf_op jit(solution)/shard_map/ppermute | solution.py:161
